TPU v7x, 512 devices: a whole 4x8x8 slice. The times are simulated.
512 devices in a mesh: gx: 64 (over x, y, z_lo), gy: 8 (over z_hi, core).
Axes of the slice: x: 4, y: 8, z: 8 (z_hi: 4, z_lo: 2; z = z_hi * 2 + z_lo), core: 2. Of those that a mesh axis runs over, the one named last changes fastest.
Arguments:
- hidden_in: bfloat16 [10, 16384], P(None, 'gx'), may hold values from -4000 to 4000
- norm_gain: bfloat16 [16384], P('gx'), may hold values from 0.099609375 to 1.8984375
- w_query: bfloat16 [16384, 16384], P('gx', 'gy'), may hold values from -0.046875 to 0.046875
- w_keyval: bfloat16 [16384, 2048], P('gx', 'gy'), may hold values from -0.09375 to 0.09375
- w_output: bfloat16 [16384, 16384], P('gx', 'gy'), may hold values from -0.1875 to 0.1875
- key_cache: bfloat16 [10, 8, 32768, 128], P(None, 'gy', 'gx'), may hold values from -1100 to 1100
- value_cache: bfloat16 [10, 8, 32768, 128], P(None, 'gy', 'gx'), may hold values from -6 to 6
- lengths: int32 [10], replicated, may hold values from 1 to 32768, as said below
Outputs:
- attn_out: bfloat16 [10, 16384], P(None, 'gy')
Inputs may be any that keep to these rules, and one draw needn't show every extreme that they name: `lengths`: some row holds 32768 positions.
All inputs are finite; a program needn't handle non-finite values.
Results may differ from a plain program's by a relative error of at most 0.012.
The roundings to bfloat16 on the way count: a program that leaves them out, or rounds other values in their place, can miss the bound.
Values may be sent and summed in bfloat16 or wider, within the bound.
A program may use at most 64 MiB of HBM per device.

v0:
```python
import jax
import jax.numpy as jnp
from jax import lax
from jax.sharding import PartitionSpec as P

D = 16384
HEADS = 128
KV = 8


def merged(array, axis, combine):
    everything = jax.tree.map(lambda part: lax.all_gather(part, axis), array)
    initial = jax.tree.map(lambda part: part[0], everything)

    def step(k, so_far):
        return combine(so_far, jax.tree.map(lambda part: part[k], everything))

    return lax.fori_loop(1, lax.axis_size(axis), step, initial)


def from_root(array, axis, root):
    mine = lax.axis_index(axis) == root
    return lax.psum(jnp.where(mine, array, jnp.zeros_like(array)), axis)


def join_partial(earlier, later):
    peak_one, weight_one, accum_one = earlier
    peak_two, weight_two, accum_two = later
    peak_both = jnp.maximum(peak_one, peak_two)
    factor_one = jnp.exp(peak_one - peak_both)
    factor_two = jnp.exp(peak_two - peak_both)
    weight_both = weight_one * factor_one + weight_two * factor_two
    accum_both = accum_one * factor_one[..., None] + accum_two * factor_two[..., None]
    return (peak_both, weight_both, accum_both)


def per_device(hidden_in, norm_gain, w_query, w_keyval, w_output, key_cache, value_cache, lengths):
    batch_rows = hidden_in.shape[0]
    kv_local = key_cache.shape[1]
    span_len = key_cache.shape[2]
    head_dim = key_cache.shape[3]
    group_size = HEADS // KV
    width_local = kv_local * group_size * head_dim
    hidden_f32 = hidden_in.astype(jnp.float32)
    scaled_in = (hidden_f32 * norm_gain.astype(jnp.float32)).astype(jnp.bfloat16)
    query_part = jnp.dot(scaled_in, w_query, preferred_element_type=jnp.float32)
    keyval_part = jnp.dot(scaled_in, w_keyval, preferred_element_type=jnp.float32)
    square_part = jnp.sum(hidden_f32 * hidden_f32, axis=1)
    query_sum, keyval_sum, square_sum = lax.psum((query_part, keyval_part, square_part), "gx")
    inv_rms = lax.rsqrt(square_sum / D + 1e-05)[:, None]
    query_flat = (query_sum * inv_rms).astype(jnp.bfloat16)
    keyval_flat = (keyval_sum * inv_rms).astype(jnp.bfloat16)
    query_new = query_flat.reshape(batch_rows, kv_local, group_size, head_dim)
    keyval_new = keyval_flat.reshape(batch_rows, kv_local, 2, head_dim)
    key_fresh = keyval_new[:, :, 0].astype(jnp.float32)
    value_fresh = keyval_new[:, :, 1].astype(jnp.float32)
    score_scale = head_dim ** (-0.5)
    score_new = (
        jnp.sum(query_new.astype(jnp.float32) * key_fresh[:, :, None, :], axis=3) * score_scale
    )
    scores = (
        jnp.einsum("bhgd,bhsd->bhgs", query_new, key_cache, preferred_element_type=jnp.float32)
        * score_scale
    )
    positions = lax.axis_index("gx") * span_len + lax.iota(jnp.int32, span_len)
    valid_pos = (positions[None, :] < lengths[:, None])[:, None, None, :]
    masked = jnp.where(valid_pos, scores, -1e30)
    peak_score = jnp.max(masked, axis=3)
    weights = jnp.where(valid_pos, jnp.exp(masked - peak_score[..., None]), 0.0)
    total_weight = jnp.sum(weights, axis=3)
    accumulated = jnp.einsum(
        "bhgs,bhsd->bhgd",
        weights.astype(jnp.bfloat16),
        value_cache,
        preferred_element_type=jnp.float32,
    )
    peak_all, weight_all, accum_all = merged(
        (peak_score, total_weight, accumulated), "gx", join_partial
    )
    top_score = jnp.maximum(peak_all, score_new)
    old_factor = jnp.exp(peak_all - top_score)
    new_factor = jnp.exp(score_new - top_score)
    denominator = weight_all * old_factor + new_factor
    numerator = (
        accum_all * old_factor[..., None] + new_factor[..., None] * value_fresh[:, :, None, :]
    )
    attn_group = (
        (numerator / denominator[..., None]).astype(jnp.bfloat16).reshape(batch_rows, width_local)
    )
    block_len = w_output.shape[0]
    per_group = lax.axis_size("gx") // lax.axis_size("gy")
    gx_index = lax.axis_index("gx")
    owner_index = gx_index // per_group
    offset = gx_index % per_group * block_len
    owned_group = from_root(attn_group, "gy", owner_index)
    own_block = lax.dynamic_slice_in_dim(owned_group, offset, block_len, 1)
    partial_out = jnp.dot(own_block, w_output, preferred_element_type=jnp.float32)
    return lax.psum(partial_out, "gx").astype(jnp.bfloat16)


def solution(mesh):
    return jax.shard_map(
        per_device,
        mesh=mesh,
        in_specs=(
            P(None, "gx"),
            P("gx"),
            P("gx", "gy"),
            P("gx", "gy"),
            P("gx", "gy"),
            P(None, "gy", "gx", None),
            P(None, "gy", "gx", None),
            P(),
        ),
        out_specs=P(None, "gy"),
        check_vma=False,
    )
```

profile of v0, /device:TPU:128, one launch (start us, length us, event | category | flops | bytes accessed | tf_op | source)
XLA Modules:
  0.0 1274.2 jit_solution(1574849001019423623)
XLA Ops:
  7.3 2.1 fusion.27
  9.9 310.3 %all-reduce = (f32[10]{0:T(128)S(1)}, f32[10,256]{1,0:T(8,128)S(1)}) all-reduce(f32[10]{0:T(128)S(1)} %fusion.22, f32[10,256]{1,0:T(8,128)S(1)} %fusion.25), channel_id=1, replica_groups=mesh['gx'=64,'gy'=8] {'gx'}, use_global_device_ids=true, to_apply=%region_2.0 | all-reduce | flops 2570 | bytes 20560 | tf_op jit(solution)/shard_map/psum | solution.py:49
  320.2 231.7 %all-reduce.3.cloned.1.call-done = f32[10,2048]{1,0:T(8,128)} async-done(((f32[10,2048]{1,0:T(8,128)}), f32[10,2048]{1,0:T(8,128)}) %all-reduce.3.cloned.1.call-update) | async-done | bytes 81936 | tf_op jit(solution)/shard_map/psum | solution.py:49
  554.9 156.4 %all-gather.4 = f32[64,10,16]{2,1,0:T(8,128)S(1)} all-gather(f32[1,10,16]{2,1,0:T(8,128)S(1)} %bitcast.90), channel_id=3, replica_groups=mesh['gx'=64,'gy'=8] {'gx'}, dimensions={0}, use_global_device_ids=true | all-gather | bytes 41600 | tf_op jit(solution)/shard_map/all_gather | solution.py:12
  711.7 153.1 %all-gather.3 = f32[64,10,16]{2,1,0:T(8,128)S(1)} all-gather(f32[1,10,16]{2,1,0:T(8,128)S(1)} %bitcast.88), channel_id=2, replica_groups=mesh['gx'=64,'gy'=8] {'gx'}, dimensions={0}, use_global_device_ids=true | all-gather | bytes 41600 | tf_op jit(solution)/shard_map/all_gather | solution.py:12
  866.3 68.9 %while.19 = (s32[]{:T(128)}, f32[10,1,16]{2,1,0:T(1,128)S(1)}, f32[10,1,16]{2,1,0:T(1,128)S(1)}, f32[10,1,16,128]{3,2,1,0:T(8,128)S(1)}, f32[64,10,1,16]{3,2,1,0...) while((s32[]{:T(128)}, f32[10,1,16]{2,1,0:T(1,128)S(1)}, ...), condition=%wide.region_6.7_spmd, body=%wide.region_5.6_spmd.sunk | while | flops 62405 | bytes 254863 | solution.py:18
  866.3 1.0 fusion.44
  868.5 1.0 fusion.44
  870.7 1.0 fusion.44
  871.8 1.0 fusion.44
  872.9 1.0 fusion.44
  874.0 1.0 fusion.44
  875.1 1.0 fusion.44
  876.2 1.0 fusion.44
  877.2 1.0 fusion.44
  878.3 1.0 fusion.44
  879.4 1.0 fusion.44
  880.5 1.0 fusion.44
  881.6 1.0 fusion.44
  882.7 1.0 fusion.44
  884.9 1.0 fusion.44
  887.1 1.0 fusion.44
  889.3 1.0 fusion.44
  891.5 1.0 fusion.44
  892.6 1.0 fusion.44
  893.7 1.0 fusion.44
  894.8 1.0 fusion.44
  895.9 1.0 fusion.44
  896.9 1.0 fusion.44
  898.0 1.0 fusion.44
  899.1 1.0 fusion.44
  900.2 1.0 fusion.44
  901.3 1.0 fusion.44
  902.4 1.0 fusion.44
  903.5 1.0 fusion.44
  905.7 1.0 fusion.44
  907.9 1.0 fusion.44
  910.1 1.0 fusion.44
  912.3 1.0 fusion.44
  913.4 1.0 fusion.44
  914.5 1.0 fusion.44
  915.5 1.0 fusion.44
  916.6 1.0 fusion.44
  917.7 1.0 fusion.44
  918.8 1.0 fusion.44
  919.9 1.0 fusion.44
  935.4 26.4 %psum.38 = bf16[10,2048]{1,0:T(8,128)(2,1)S(1)} all-reduce(bf16[10,2048]{1,0:T(8,128)(2,1)S(1)} %bitcast.86), channel_id=1, replica_groups=mesh['gx'=64,'gy'=8] {'gy'}, use_global_device_ids=true, to_apply=%region_9.10 | all-reduce | flops 20480 | bytes 81920 | tf_op jit(solution)/shard_map/psum | solution.py:23
  962.1 305.2 %psum.39 = bf16[10,2048]{1,0:T(8,128)(2,1)} all-reduce(f32[10,2048]{1,0:T(8,128)S(1)} %fusion.23), channel_id=1, replica_groups=mesh['gx'=64,'gy'=8] {'gx'}, use_global_device_ids=true, to_apply=%region_10.11 | all-reduce | flops 20480 | bytes 122880 | tf_op jit(solution)/shard_map/psum | solution.py:98
  (199 shorter events, 32.4 us)
Async XLA Ops:
  6.5 546.4 %copy-start = (bf16[10,1,512,128]{3,2,1,0:T(8,128)(2,1)S(1)}, bf16[10,1,512,128]{3,2,1,0:T(8,128)(2,1)}, u32[]{:S(2)}) copy-start(bf16[10,1,512,128]{3,2,1,0:T(8,128)(2,1)} %param.15) | copy-start | bytes 3932164
  6.5 3.0 copy-start.4
  6.5 3.2 copy-start.3
  6.5 3.3 copy-start.5
  6.5 545.4 %all-reduce.3.cloned.1.call-start = ((), (), s32[]{:S(2)}) async-start(), calls=%async_computation | async-start | bytes 262144 | tf_op jit(solution)/shard_map/psum | solution.py:49
  9.5 543.9 %copy-start.1 = (bf16[10,1,512,128]{3,2,1,0:T(8,128)(2,1)S(1)}, bf16[10,1,512,128]{3,2,1,0:T(8,128)(2,1)}, u32[]{:S(2)}) copy-start(bf16[10,1,512,128]{3,2,1,0:T(8,128)(2,1)} %param.16) | copy-start | bytes 3932164
  9.5 855.7 %all-gather.7.cloned.1.call-start = ((), (), s32[]{:S(2)}) async-start(), calls=%async_computation.1 | async-start | bytes 5324800 | tf_op jit(solution)/shard_map/all_gather | solution.py:12
  865.3 96.6 %copy-start.2 = (bf16[256,2048]{1,0:T(8,128)(2,1)S(1)}, bf16[256,2048]{1,0:T(8,128)(2,1)}, u32[]{:S(2)}) copy-start(bf16[256,2048]{1,0:T(8,128)(2,1)} %param.14) | copy-start | bytes 3145732
Sparse Core Ops, SparseCore 0:
  10.3 541.5 all-reduce.2
  554.6 305.2 all-gather.6
where the time goes:
time: 1280 us; the launch traced here: 1270 us
  blocking collectives  951 us (74%)
  waiting for transfers between devices  232 us (18%)
  other arithmetic  68.9 us (5%)
  between operations  13.6 us (1%)
    psum x1, blocking collectives, per_device(): lax.psum((query_part, keyval_part, square_part), 'gx')  310 us
    all_gather x2, blocking collectives, merged(): everything = jax.tree.map(lambda part: lax.all_gather(part, axis), array)  310 us
    psum x1, blocking collectives, per_device(): return lax.psum(partial_out, 'gx').astype(jnp.bfloat16)  305 us
    psum x1, waiting for transfers between devices, per_device(): lax.psum((query_part, keyval_part, square_part), 'gx')  232 us
    add x63, other arithmetic, join_partial(): accum_one * factor_one[..., None] + accum_two * factor_two[..., None]  64 us
    psum x1, blocking collectives, from_root(): return lax.psum(jnp.where(mine, array, jnp.zeros_like(array)), axis)  26.4 us
  transfers between devices with their start and end apart: 2, of which 1 were waited for; matrix products, arithmetic and copies ran while one was open for 0% of the time, Pallas kernels for 0%

commit v1 on v0

v1 whole, which is shorter than its diff:
```python
import functools

import jax
import jax.numpy as jnp
from jax import lax
from jax.experimental import pallas as pl
from jax.experimental.pallas import tpu as pltpu
from jax.sharding import PartitionSpec as P

D = 16384
HEADS = 128
KV = 8
HD = 128
ROWS = 10
GROUP = HEADS // KV
SPAN = 512
NX = 64
NY = 8
MESH = pl.DeviceIdType.MESH

Q_UNITS = ROWS * GROUP
KEY_UNIT = Q_UNITS
VALUE_UNIT = KEY_UNIT + ROWS
SQUARE_UNIT = VALUE_UNIT + ROWS
IN_BLOCKS = (SQUARE_UNIT + ROWS + 3) // 4
OUT_BLOCKS = Q_UNITS // 4
HALF = ROWS // 2


def offset(index, size):
    return size // 2 + (1 - 2 * (index % 2)) * ((index + 1) // 2)


def peer(index, gx):
    dy, dx, dz = offset(index // 8, 8), offset((index // 2) % 4, 4), 1 - index % 2
    x, y, z = gx // 16, (gx // 2) % 8, gx % 2
    return ((x + dx) % 4) * 16 + ((y + dy) % 8) * 2 + (z + dz) % 2


def put_unit(ref, unit, value):
    ref[unit // 4, pl.ds(unit % 4, 1), :] = value


def await_bytes(ref, sem):
    pltpu.make_async_copy(ref, ref, sem).wait()


def kernel(
    hidden_ref, gain_ref, w_query_hbm, w_keyval_hbm, w_output_hbm, key_hbm, value_hbm, lengths_ref,
    out_ref,
    w_query, w_keyval, w_output, keys, values,
    in_send, in_recv, in_sum, in_all,
    soft_send, soft_recv, attn_send, attn_recv,
    out_send, out_recv, out_sum,
    load_sem, send_sem, recv_sem,
):
    gx, gy = lax.axis_index("gx"), lax.axis_index("gy")
    merges = (gx // 8) % 2 == gy % 2
    soft_block = (2 * (gx % 8) + gx // 32) * 2 + (gx // 16) % 2
    attn_gx = gy * 8 + gx % 8
    home = gx // 8

    barrier = pltpu.get_barrier_semaphore()

    def greet(index, carry):
        pl.semaphore_signal(barrier, inc=1, device_id=(peer(index, gx), gy), device_id_type=MESH)
        return carry

    lax.fori_loop(0, NX - 1, greet, 0)

    @pl.when(gy != home)
    def _():
        def greet_merger(index, carry):
            merger = index * 16 + (home % 2) * 8 + gx % 8
            pl.semaphore_signal(barrier, inc=1, device_id=(merger, home), device_id_type=MESH)
            return carry

        lax.fori_loop(0, 4, greet_merger, 0)

    loads = [
        pltpu.make_async_copy(src, dst, load_sem.at[k])
        for k, (src, dst) in enumerate(
            [
                (w_query_hbm, w_query),
                (w_keyval_hbm, w_keyval),
                (key_hbm, keys),
                (value_hbm, values),
                (w_output_hbm, w_output),
            ]
        )
    ]
    for load in loads:
        load.start()

    def reduce_blocks(stage, blocks, send, recv, total):
        mine = gx < blocks

        def send_block(index, carry):
            target = peer(index, gx)

            @pl.when(target < blocks)
            def _():
                pltpu.make_async_remote_copy(
                    src_ref=send.at[target], dst_ref=recv.at[gx],
                    send_sem=send_sem.at[stage], recv_sem=recv_sem.at[stage],
                    device_id=(target, gy), device_id_type=MESH,
                ).start()

            return carry

        lax.fori_loop(0, NX - 1, send_block, 0)

        @pl.when(mine)
        def _():
            recv[gx] = send[gx]
            await_bytes(recv.at[pl.ds(0, NX - 1)], recv_sem.at[stage])
            total[...] = jnp.sum(recv[...], axis=0)

    def spread_blocks(stage, blocks, total, everything):
        mine = gx < blocks

        @pl.when(mine)
        def _():
            def send_total(index, carry):
                pltpu.make_async_remote_copy(
                    src_ref=total, dst_ref=everything.at[gx],
                    send_sem=send_sem.at[stage], recv_sem=recv_sem.at[stage],
                    device_id=(peer(index, gx), gy), device_id_type=MESH,
                ).start()
                return carry

            lax.fori_loop(0, NX - 1, send_total, 0)
            everything[gx] = total[...]
            await_bytes(everything.at[pl.ds(0, blocks - 1)], recv_sem.at[stage])

        @pl.when(jnp.logical_not(mine))
        def _():
            await_bytes(everything.at[pl.ds(0, blocks)], recv_sem.at[stage])

    hidden = hidden_ref[...].astype(jnp.float32)
    squares = jnp.broadcast_to(jnp.sum(hidden * hidden, axis=1, keepdims=True), (ROWS, HD))
    scaled_in = (hidden * gain_ref[...].astype(jnp.float32)).astype(jnp.bfloat16)
    loads[0].wait()
    query_part = jnp.dot(scaled_in, w_query[...], preferred_element_type=jnp.float32)
    for r in range(ROWS):
        for h in range(GROUP):
            put_unit(in_send, r * GROUP + h, query_part[r : r + 1, h * HD : (h + 1) * HD])
    loads[1].wait()
    keyval_part = jnp.dot(scaled_in, w_keyval[...], preferred_element_type=jnp.float32)
    for r in range(ROWS):
        put_unit(in_send, KEY_UNIT + r, keyval_part[r : r + 1, :HD])
        put_unit(in_send, VALUE_UNIT + r, keyval_part[r : r + 1, HD:])
        put_unit(in_send, SQUARE_UNIT + r, squares[r : r + 1])
    for unit in range(SQUARE_UNIT + ROWS, IN_BLOCKS * 4):
        put_unit(in_send, unit, jnp.zeros((1, HD), jnp.float32))

    @pl.when(merges)
    def _():
        pl.semaphore_wait(barrier, NX - 1 + NY - 1)

    @pl.when(jnp.logical_not(merges))
    def _():
        pl.semaphore_wait(barrier, NX - 1)

    reduce_blocks(0, IN_BLOCKS, in_send, in_recv, in_sum)
    spread_blocks(1, IN_BLOCKS, in_sum, in_all)

    def unit(index):
        return in_all[index // 4, index % 4 : index % 4 + 1, :]

    loads[2].wait()
    loads[3].wait()
    score_scale = HD ** (-0.5)
    position = gx * SPAN + lax.broadcasted_iota(jnp.int32, (GROUP, SPAN), 1)
    lane = lax.broadcasted_iota(jnp.int32, (GROUP, HD), 1)
    first = gx == 0
    for half in range(2):
        peaks = jnp.zeros((GROUP, HD), jnp.float32)
        totals = jnp.zeros((GROUP, HD), jnp.float32)
        for k in range(HALF):
            r = half * HALF + k
            inv_rms = lax.rsqrt(unit(SQUARE_UNIT + r) / D + 1e-05)
            query = in_all[r * 4 : r * 4 + 4].reshape(GROUP, HD)
            query = (query * inv_rms).astype(jnp.bfloat16)
            key_new = (unit(KEY_UNIT + r) * inv_rms).astype(jnp.bfloat16).astype(jnp.float32)
            value_new = (unit(VALUE_UNIT + r) * inv_rms).astype(jnp.bfloat16).astype(jnp.float32)
            score_new = (
                jnp.sum(query.astype(jnp.float32) * key_new, axis=1, keepdims=True) * score_scale
            )
            score_new = jnp.where(first, score_new, -1e30)
            scores = (
                lax.dot_general(
                    query, keys[r, 0], (((1,), (1,)), ((), ())), preferred_element_type=jnp.float32
                )
                * score_scale
            )
            valid = position < lengths_ref[r]
            masked = jnp.where(valid, scores, -1e30)
            peak = jnp.maximum(jnp.max(masked, axis=1, keepdims=True), score_new)
            weights = jnp.where(valid, jnp.exp(masked - peak), 0.0)
            fresh = jnp.where(first, jnp.exp(score_new - peak), 0.0)
            total = jnp.sum(weights, axis=1, keepdims=True) + fresh
            accum = jnp.dot(
                weights.astype(jnp.bfloat16), values[r, 0], preferred_element_type=jnp.float32
            )
            accum = accum + fresh * value_new
            for h in range(GROUP):
                soft_send[h * 2 + half, k : k + 1, :] = accum[h : h + 1]
            peaks = jnp.where(lane == k, peak, peaks)
            totals = jnp.where(lane == k, total, totals)
        for h in range(GROUP):
            soft_send[h * 2 + half, HALF : HALF + 1, :] = peaks[h : h + 1]
            soft_send[h * 2 + half, HALF + 1 : HALF + 2, :] = totals[h : h + 1]
            soft_send[h * 2 + half, HALF + 2 : HALF + 3, :] = jnp.zeros((1, HD), jnp.float32)

    def send_soft(index, carry):
        target = peer(index, gx)

        @pl.when((target // 8) % 2 == gy % 2)
        def _():
            block = (2 * (target % 8) + target // 32) * 2 + (target // 16) % 2
            pltpu.make_async_remote_copy(
                src_ref=soft_send.at[block], dst_ref=soft_recv.at[gx],
                send_sem=send_sem.at[2], recv_sem=recv_sem.at[2],
                device_id=(target, gy), device_id_type=MESH,
            ).start()

        return carry

    lax.fori_loop(0, NX - 1, send_soft, 0)

    @pl.when(merges)
    def _():
        soft_recv[gx] = soft_send[soft_block]
        await_bytes(soft_recv.at[pl.ds(0, NX - 1)], recv_sem.at[2])
        peaks = soft_recv[:, HALF, :]
        factors = jnp.exp(peaks - jnp.max(peaks, axis=0, keepdims=True))
        totals = jnp.sum(factors * soft_recv[:, HALF + 1, :], axis=0, keepdims=True)
        for k in range(HALF):
            weighted = jnp.sum(factors[:, k : k + 1] * soft_recv[:, k, :], axis=0, keepdims=True)
            attention = (weighted / totals[:, k : k + 1]).astype(jnp.bfloat16)
            attn_send[k : k + 1, :] = attention.astype(jnp.float32)
        attn_send[HALF:, :] = jnp.zeros((8 - HALF, HD), jnp.float32)

        def send_attention(index, carry):
            column = (gy + 4 + index) % NY

            @pl.when((column != gy) | (attn_gx != gx))
            def _():
                pltpu.make_async_remote_copy(
                    src_ref=attn_send, dst_ref=attn_recv.at[gx // 16],
                    send_sem=send_sem.at[3], recv_sem=recv_sem.at[3],
                    device_id=(attn_gx, column), device_id_type=MESH,
                ).start()

            return carry

        lax.fori_loop(0, NY, send_attention, 0)

    @pl.when(gy == home)
    def _():
        attn_recv[gx // 16] = attn_send[...]
        await_bytes(attn_recv.at[pl.ds(0, 3)], recv_sem.at[3])

    @pl.when(gy != home)
    def _():
        await_bytes(attn_recv, recv_sem.at[3])

    loads[4].wait()
    attention = jnp.concatenate(
        [
            jnp.concatenate([attn_recv[half], attn_recv[2 + half]], axis=1)
            for half in range(2)
        ],
        axis=0,
    ).astype(jnp.bfloat16)
    out_part = jnp.dot(attention, w_output[...], preferred_element_type=jnp.float32)
    for r in range(ROWS):
        row = r // HALF * 8 + r % HALF
        for c in range(GROUP):
            put_unit(out_send, r * GROUP + c, out_part[row : row + 1, c * HD : (c + 1) * HD])
    reduce_blocks(4, OUT_BLOCKS, out_send, out_recv, out_sum)
    spread_blocks(5, OUT_BLOCKS, out_sum, out_ref)

    def await_sends(stage, sender, ref, count):
        @pl.when(sender)
        def _():
            await_bytes(ref.at[pl.ds(0, count)], send_sem.at[stage])

    await_sends(0, gx < IN_BLOCKS, in_recv, IN_BLOCKS - 1)
    await_sends(0, gx >= IN_BLOCKS, in_recv, IN_BLOCKS)
    await_sends(1, gx < IN_BLOCKS, in_recv, NX - 1)
    await_sends(2, merges, soft_recv, 31)
    await_sends(2, jnp.logical_not(merges), soft_recv, 32)
    await_sends(3, merges & (attn_gx == gx), soft_recv, NY - 1)
    await_sends(3, merges & (attn_gx != gx), soft_recv, NY)
    await_sends(4, gx < OUT_BLOCKS, in_recv, OUT_BLOCKS - 1)
    await_sends(4, gx >= OUT_BLOCKS, in_recv, OUT_BLOCKS)
    await_sends(5, gx < OUT_BLOCKS, in_recv, NX - 1)


def per_device(hidden_in, norm_gain, w_query, w_keyval, w_output, key_cache, value_cache, lengths):
    vmem = pl.BlockSpec(memory_space=pltpu.VMEM)
    hbm = pl.BlockSpec(memory_space=pl.ANY)
    block = (4, HD)
    scratch = [
        pltpu.VMEM(w_query.shape, jnp.bfloat16),
        pltpu.VMEM(w_keyval.shape, jnp.bfloat16),
        pltpu.VMEM(w_output.shape, jnp.bfloat16),
        pltpu.VMEM(key_cache.shape, jnp.bfloat16),
        pltpu.VMEM(value_cache.shape, jnp.bfloat16),
        pltpu.VMEM((IN_BLOCKS, *block), jnp.float32),
        pltpu.VMEM((NX, *block), jnp.float32),
        pltpu.VMEM(block, jnp.float32),
        pltpu.VMEM((IN_BLOCKS, *block), jnp.float32),
        pltpu.VMEM((2 * GROUP, 8, HD), jnp.float32),
        pltpu.VMEM((NX, 8, HD), jnp.float32),
        pltpu.VMEM((8, HD), jnp.float32),
        pltpu.VMEM((4, 8, HD), jnp.float32),
        pltpu.VMEM((OUT_BLOCKS, *block), jnp.float32),
        pltpu.VMEM((NX, *block), jnp.float32),
        pltpu.VMEM(block, jnp.float32),
        pltpu.SemaphoreType.DMA((5,)),
        pltpu.SemaphoreType.DMA((6,)),
        pltpu.SemaphoreType.DMA((6,)),
    ]
    out = pl.pallas_call(
        kernel,
        out_shape=jax.ShapeDtypeStruct((OUT_BLOCKS, *block), jnp.float32),
        in_specs=[vmem, vmem, hbm, hbm, hbm, hbm, hbm, pl.BlockSpec(memory_space=pltpu.SMEM)],
        out_specs=vmem,
        scratch_shapes=scratch,
        compiler_params=pltpu.CompilerParams(
            collective_id=0, has_side_effects=True, vmem_limit_bytes=60 * 2**20
        ),
        cost_estimate=pl.CostEstimate(flops=64 * 2**20, bytes_accessed=5 * 2**20, transcendentals=81920),
    )(hidden_in, norm_gain.reshape(1, -1), w_query, w_keyval, w_output, key_cache, value_cache, lengths)
    return out.reshape(ROWS, GROUP * HD).astype(jnp.bfloat16)


def solution(mesh):
    return jax.shard_map(
        per_device,
        mesh=mesh,
        in_specs=(
            P(None, "gx"),
            P("gx"),
            P("gx", "gy"),
            P("gx", "gy"),
            P("gx", "gy"),
            P(None, "gy", "gx", None),
            P(None, "gy", "gx", None),
            P(),
        ),
        out_specs=P(None, "gy"),
        check_vma=False,
    )
```

time: 1280 us -> 65.4 us (0.05)
  the two profiles are of different devices: /device:TPU:128 before, /device:TPU:6 now
where the time goes in v1:
time: 65.4 us; the launch traced here: 64.6 us
  Pallas kernels  61.8 us (94%)
  local copies, waits for them, and re-layouts  1.87 us (3%)
  other arithmetic  0.9 us (1%)
    pallas_call x1, Pallas kernels, per_device(): pl.pallas_call(kernel, out_shape=jax.ShapeDtypeStruct((OUT_BLOCKS, *block...  61.8 us

profile of v1, /device:TPU:6, one launch (start us, length us, event | category | flops | bytes accessed | tf_op | source)
XLA Modules:
  0.0 64.6 jit_solution(15186207866000363364)
XLA Ops:
  0.0 1.2 %reshape.5.gain_ref = bf16[1,256]{1,0:T(2,128)(2,1)} reshape(bf16[256]{0:T(256)(128)(2,1)} %param.9) | data formatting | bytes 1024 | tf_op jit(solution)/shard_map/reshape | solution.py:337
  1.2 61.8 %shard_map.82 = f32[40,4,128]{2,1,0:T(4,128)} custom-call(bf16[10,256]{1,0:T(8,128)(2,1)} %hidden_ref.1, bf16[1,256]{1,0:T(2,128)(2,1)} %reshape.5.gain_ref, bf16[256,2048]{1,0:T(8,128)(2,1)} %w_query_hbm.1, bf16[256,256]{1,0:T(8,128)(2,1)} %w_keyval_hbm.1, bf16[256,2048]{1,0:T(8,128)(2,1)} %w_output_hbm.1, bf16[10,1,512,128]{3,2,1,0:T(8,128)(2,1)} %key_hbm.1, ...), custom_call_target="tpu_custom_call" | custom-call | flops 67108864 | bytes 5242880 | tf_op jit(solution)/shard_map/pallas_call | solution.py:327
  63.0 0.9 %convert_element_type.6 = bf16[40,4,128]{2,1,0:T(4,128)(2,1)S(1)} convert(f32[40,4,128]{2,1,0:T(4,128)} %shard_map.82) | non-fusion elementwise | flops 20480 | bytes 122880 | tf_op jit(solution)/shard_map/convert_element_type | solution.py:338
  63.9 0.7 %convert_element_type.7 = bf16[10,2048]{1,0:T(8,128)(2,1)} reshape(bf16[40,4,128]{2,1,0:T(4,128)(2,1)S(1)} %convert_element_type.6) | data formatting | bytes 81920 | tf_op jit(solution)/shard_map/convert_element_type | solution.py:338

commit v2 on v0

v2 whole, which is shorter than its diff:
```python
import jax
import jax.numpy as jnp
from jax import lax
from jax.experimental import pallas as pl
from jax.experimental.pallas import tpu as pltpu
from jax.sharding import PartitionSpec as P

D = 16384
HEADS = 128
KV = 8
HD = 128
ROWS = 10
GROUP = HEADS // KV
SPAN = 512
MESH = pl.DeviceIdType.MESH

SLICES = 8
PAIR = 2 * ROWS
BLOCK = PAIR + 4
PEAK = PAIR
TOTAL = PAIR + 1


def offset(index, size):
    return size // 2 + (1 - 2 * (index % 2)) * ((index + 1) // 2)


def await_bytes(ref, sem):
    pltpu.make_async_copy(ref, ref, sem).wait()


def merge_partials(blocks, count):
    peaks = blocks[:, PEAK, :]
    peak = jnp.max(peaks, axis=0, keepdims=True)
    factors = jnp.exp(peaks - peak)
    total = jnp.sum(factors * blocks[:, TOTAL, :], axis=0, keepdims=True)
    if count < 8:
        factors = jnp.concatenate([factors, jnp.broadcast_to(total, (8 - count, HD))], axis=0)
    columns = jnp.transpose(factors)
    accum = columns[:BLOCK, 0:1] * blocks[0]
    for k in range(1, count):
        accum = accum + columns[:BLOCK, k : k + 1] * blocks[k]
    return accum, peak, total, columns


def kernel(
    hidden_hbm, gain_hbm, w_query_hbm, w_keyval_hbm, w_output_hbm, key_hbm, value_hbm, lengths_ref,
    out_ref,
    hidden_in, norm_gain, w_query, w_keyval, w_output, keys, values,
    in_send, in_plane, in_mid, in_line, in_sum, in_all,
    soft_send, soft_recv, soft_mid, attn_recv,
    out_send, out_plane, out_mid, out_line, out_sum, out_all,
    load_sem, send_sem, recv_sem,
):
    gx, gy = lax.axis_index("gx"), lax.axis_index("gy")
    x, y, z = gx // 16, (gx // 2) % 8, gx % 2
    plane = x * 2 + z
    merges = y // 4 == gy % 2
    source_gy = 2 * x + y // 4

    def place(x, y, z):
        return x * 16 + y * 2 + z

    def plane_mate(index):
        return (x + offset(index // 2, 4)) % 4, (z + 1 - index % 2) % 2

    def line_mate(index):
        return (y + offset(index, 8)) % 8

    barrier = pltpu.get_barrier_semaphore()

    def signal(gx_to, gy_to):
        pl.semaphore_signal(barrier, inc=1, device_id=(gx_to, gy_to), device_id_type=MESH)

    @pl.when(source_gy != gy)
    def _():
        def greet_source(index, carry):
            signal(place(index, y, z), source_gy)
            return carry

        lax.fori_loop(0, 4, greet_source, 0)

    def greet(index, carry):
        x_mate, z_mate = plane_mate(index)
        y_mate = line_mate(index)
        signal(place(x, y_mate, 1 - z), gy)
        signal(place(x, y_mate, z), gy)
        signal(place(x_mate, y, z_mate), gy)
        return carry

    lax.fori_loop(0, 7, greet, 0)

    loads = [
        pltpu.make_async_copy(src, dst, load_sem.at[k])
        for k, (src, dst) in enumerate(
            [
                (hidden_hbm, hidden_in),
                (gain_hbm, norm_gain),
                (w_query_hbm, w_query),
                (w_keyval_hbm, w_keyval),
                (key_hbm, keys),
                (value_hbm, values),
                (w_output_hbm, w_output),
            ]
        )
    ]
    for load in loads:
        load.start()

    def copy(stage, src, dst, gx_to, gy_to):
        pltpu.make_async_remote_copy(
            src_ref=src, dst_ref=dst, send_sem=send_sem.at[stage], recv_sem=recv_sem.at[stage],
            device_id=(gx_to, gy_to), device_id_type=MESH,
        ).start()

    def all_reduce(stage, send, by_plane, mid, by_line, total, everything):
        def to_plane(index, carry):
            x_mate, z_mate = plane_mate(index)
            copy(stage, send.at[x_mate * 2 + z_mate], by_plane.at[plane], place(x_mate, y, z_mate), gy)
            return carry

        lax.fori_loop(0, 7, to_plane, 0)
        by_plane[plane] = send[plane]
        await_bytes(by_plane.at[pl.ds(0, 7)], recv_sem.at[stage])
        mid[...] = jnp.sum(by_plane[...], axis=0)

        def to_line(index, carry):
            copy(stage + 1, mid, by_line.at[y], place(x, line_mate(index), z), gy)
            return carry

        lax.fori_loop(0, 7, to_line, 0)
        by_line[y] = mid[...]
        await_bytes(by_line.at[pl.ds(0, 7)], recv_sem.at[stage + 1])
        total[...] = jnp.sum(by_line[...], axis=0)

        def back_to_plane(index, carry):
            x_mate, z_mate = plane_mate(index)
            copy(stage + 2, total, everything.at[plane], place(x_mate, y, z_mate), gy)
            return carry

        lax.fori_loop(0, 7, back_to_plane, 0)
        everything[plane] = total[...]
        await_bytes(everything.at[pl.ds(0, 7)], recv_sem.at[stage + 2])

    loads[0].wait()
    loads[1].wait()
    hidden = hidden_in[...].astype(jnp.float32)
    squares = jnp.broadcast_to(jnp.sum(hidden * hidden, axis=1, keepdims=True), (ROWS, HD))
    gain = norm_gain[...].astype(jnp.float32).reshape(1, -1)
    scaled_in = (hidden * gain).astype(jnp.bfloat16)
    loads[2].wait()
    query_part = jnp.dot(scaled_in, w_query[...], preferred_element_type=jnp.float32)
    for j in range(SLICES):
        in_send[j, :ROWS, :] = query_part[:, j * 2 * HD : (j * 2 + 1) * HD]
        in_send[j, ROWS:PAIR, :] = query_part[:, (j * 2 + 1) * HD : (j * 2 + 2) * HD]
    loads[3].wait()
    keyval_part = jnp.dot(scaled_in, w_keyval[...], preferred_element_type=jnp.float32)
    extras = [keyval_part[:, :HD], keyval_part[:, HD:], squares, jnp.zeros((2, HD), jnp.float32)]
    slot = 0
    for extra in extras:
        for r in range(extra.shape[0]):
            in_send[slot // 4, PAIR + slot % 4 : PAIR + slot % 4 + 1, :] = extra[r : r + 1]
            slot += 1

    @pl.when(merges)
    def _():
        pl.semaphore_wait(barrier, 21 + 7)

    @pl.when(jnp.logical_not(merges))
    def _():
        pl.semaphore_wait(barrier, 21)

    all_reduce(0, in_send, in_plane, in_mid, in_line, in_sum, in_all)

    def extra_row(kind, r):
        slot = kind * ROWS + r
        return in_all[slot // 4, PAIR + slot % 4 : PAIR + slot % 4 + 1, :]

    loads[4].wait()
    score_scale = HD ** (-0.5)
    position = gx * SPAN + lax.broadcasted_iota(jnp.int32, (GROUP, SPAN), 1)
    first = gx == 0
    queries, scores, values_new, scores_new = [], [], [], []
    for r in range(ROWS):
        inv_rms = lax.rsqrt(extra_row(2, r) / D + 1e-05)
        query = jnp.concatenate([in_all[:, r, :], in_all[:, ROWS + r, :]], axis=0)
        query = (query * inv_rms).astype(jnp.bfloat16)
        key_new = (extra_row(0, r) * inv_rms).astype(jnp.bfloat16).astype(jnp.float32)
        values_new.append((extra_row(1, r) * inv_rms).astype(jnp.bfloat16).astype(jnp.float32))
        score_new = (
            jnp.sum(query.astype(jnp.float32) * key_new, axis=1, keepdims=True) * score_scale
        )
        scores_new.append(jnp.where(first, score_new, -1e30))
        scores.append(
            lax.dot_general(
                query, keys[r, 0], (((1,), (1,)), ((), ())), preferred_element_type=jnp.float32
            )
            * score_scale
        )
    loads[5].wait()
    head_row = lax.broadcasted_iota(jnp.int32, (GROUP, HD), 0)
    lane = lax.broadcasted_iota(jnp.int32, (GROUP, HD), 1) - ROWS * (head_row // SLICES)
    peaks = jnp.zeros((GROUP, HD), jnp.float32)
    totals = jnp.zeros((GROUP, HD), jnp.float32)
    for r in range(ROWS):
        valid = position < lengths_ref[r]
        masked = jnp.where(valid, scores[r], -1e30)
        peak = jnp.maximum(jnp.max(masked, axis=1, keepdims=True), scores_new[r])
        weights = jnp.where(valid, jnp.exp(masked - peak), 0.0)
        fresh = jnp.where(first, jnp.exp(scores_new[r] - peak), 0.0)
        total = jnp.sum(weights, axis=1, keepdims=True) + fresh
        accum = jnp.dot(
            weights.astype(jnp.bfloat16), values[r, 0], preferred_element_type=jnp.float32
        )
        accum = accum + fresh * values_new[r]
        soft_send[:, r, :] = accum[:SLICES]
        soft_send[:, ROWS + r, :] = accum[SLICES:]
        peaks = jnp.where(lane == r, peak, peaks)
        totals = jnp.where(lane == r, total, totals)
    soft_send[:, PEAK, :] = peaks[:SLICES] + peaks[SLICES:]
    soft_send[:, TOTAL, :] = totals[:SLICES] + totals[SLICES:]
    soft_send[:, TOTAL + 1, :] = jnp.zeros((SLICES, HD), jnp.float32)
    soft_send[:, TOTAL + 2, :] = jnp.zeros((SLICES, HD), jnp.float32)

    def to_merger(index, carry):
        y_to, z_to = (gy % 2) * 4 + index // 2, index % 2

        @pl.when((y_to != y) | (z_to != z))
        def _():
            copy(3, soft_send.at[index], soft_recv.at[y * 2 + z], place(x, y_to, z_to), gy)

        return carry

    lax.fori_loop(0, SLICES, to_merger, 0)

    @pl.when(merges)
    def _():
        soft_recv[y * 2 + z] = soft_send[(y % 4) * 2 + z]
        await_bytes(soft_recv.at[pl.ds(0, 15)], recv_sem.at[3])
        accum, peak, total, _ = merge_partials(soft_recv, 16)
        soft_mid[...] = accum
        soft_mid[PEAK : PEAK + 1, :] = peak
        soft_mid[TOTAL : TOTAL + 1, :] = total

        def to_outputs(index, carry):
            gy_to = (gy + 4 + index) % 8

            @pl.when((gy_to != gy) | (x != gy // 2))
            def _():
                copy(4, soft_mid, attn_recv.at[x], place(gy // 2, y, z), gy_to)

            return carry

        lax.fori_loop(0, 8, to_outputs, 0)

    @pl.when(source_gy == gy)
    def _():
        attn_recv[x] = soft_mid[...]
        await_bytes(attn_recv.at[pl.ds(0, 3)], recv_sem.at[4])

    @pl.when(source_gy != gy)
    def _():
        await_bytes(attn_recv, recv_sem.at[4])

    accum, _, _, columns = merge_partials(attn_recv, 4)
    attention = (accum[:PAIR] / columns[:PAIR, 4:5]).astype(jnp.bfloat16)
    attention = jnp.concatenate([attention[:ROWS], attention[ROWS:]], axis=1)
    loads[6].wait()
    out_part = jnp.dot(attention, w_output[...], preferred_element_type=jnp.float32)
    for j in range(SLICES):
        out_send[j, :ROWS, :] = out_part[:, j * 2 * HD : (j * 2 + 1) * HD]
        out_send[j, ROWS:, :] = out_part[:, (j * 2 + 1) * HD : (j * 2 + 2) * HD]
    all_reduce(5, out_send, out_plane, out_mid, out_line, out_sum, out_all)
    for j in range(SLICES):
        out_ref[:, j * 2 * HD : (j * 2 + 1) * HD] = out_all[j, :ROWS, :]
        out_ref[:, (j * 2 + 1) * HD : (j * 2 + 2) * HD] = out_all[j, ROWS:, :]

    for stage in range(3):
        await_bytes(in_all.at[pl.ds(0, 7)], send_sem.at[stage])
        await_bytes(out_all.at[pl.ds(0, 7)], send_sem.at[5 + stage])

    @pl.when(merges)
    def _():
        await_bytes(soft_recv.at[pl.ds(0, 7)], send_sem.at[3])

    @pl.when(jnp.logical_not(merges))
    def _():
        await_bytes(soft_recv.at[pl.ds(0, 8)], send_sem.at[3])

    @pl.when(merges & (x == gy // 2))
    def _():
        await_bytes(soft_recv.at[pl.ds(0, 7)], send_sem.at[4])

    @pl.when(merges & (x != gy // 2))
    def _():
        await_bytes(soft_recv.at[pl.ds(0, 8)], send_sem.at[4])


def per_device(hidden_in, norm_gain, w_query, w_keyval, w_output, key_cache, value_cache, lengths):
    hbm = pl.BlockSpec(memory_space=pl.ANY)

    def reduction(rows):
        return [
            pltpu.VMEM((SLICES, rows, HD), jnp.float32),
            pltpu.VMEM((SLICES, rows, HD), jnp.float32),
            pltpu.VMEM((rows, HD), jnp.float32),
            pltpu.VMEM((SLICES, rows, HD), jnp.float32),
            pltpu.VMEM((rows, HD), jnp.float32),
            pltpu.VMEM((SLICES, rows, HD), jnp.float32),
        ]

    scratch = [
        pltpu.VMEM(hidden_in.shape, jnp.bfloat16),
        pltpu.VMEM(norm_gain.shape, jnp.bfloat16),
        pltpu.VMEM(w_query.shape, jnp.bfloat16),
        pltpu.VMEM(w_keyval.shape, jnp.bfloat16),
        pltpu.VMEM(w_output.shape, jnp.bfloat16),
        pltpu.VMEM(key_cache.shape, jnp.bfloat16),
        pltpu.VMEM(value_cache.shape, jnp.bfloat16),
        *reduction(BLOCK),
        pltpu.VMEM((SLICES, BLOCK, HD), jnp.float32),
        pltpu.VMEM((16, BLOCK, HD), jnp.float32),
        pltpu.VMEM((BLOCK, HD), jnp.float32),
        pltpu.VMEM((4, BLOCK, HD), jnp.float32),
        *reduction(PAIR),
        pltpu.SemaphoreType.DMA((7,)),
        pltpu.SemaphoreType.DMA((8,)),
        pltpu.SemaphoreType.DMA((8,)),
    ]
    out = pl.pallas_call(
        kernel,
        out_shape=jax.ShapeDtypeStruct((ROWS, GROUP * HD), jnp.float32),
        in_specs=[hbm] * 7 + [pl.BlockSpec(memory_space=pltpu.SMEM)],
        out_specs=pl.BlockSpec(memory_space=pltpu.VMEM),
        scratch_shapes=scratch,
        compiler_params=pltpu.CompilerParams(
            collective_id=0, has_side_effects=True, vmem_limit_bytes=60 * 2**20
        ),
    )(hidden_in, norm_gain, w_query, w_keyval, w_output, key_cache, value_cache, lengths)
    return out.astype(jnp.bfloat16)


def solution(mesh):
    return jax.shard_map(
        per_device,
        mesh=mesh,
        in_specs=(
            P(None, "gx"),
            P("gx"),
            P("gx", "gy"),
            P("gx", "gy"),
            P("gx", "gy"),
            P(None, "gy", "gx", None),
            P(None, "gy", "gx", None),
            P(),
        ),
        out_specs=P(None, "gy"),
        check_vma=False,
    )
```

time: 1280 us -> 54.5 us (0.04)
  the two profiles are of different devices: /device:TPU:128 before, /device:TPU:6 now
where the time goes in v2:
time: 54.5 us; the launch traced here: 54.4 us
  Pallas kernels  52.8 us (97%)
  other arithmetic  1.54 us (3%)
    pallas_call x1, Pallas kernels, per_device(): pl.pallas_call(kernel, out_shape=jax.ShapeDtypeStruct((ROWS, GROUP * HD),...  52.8 us
    convert_element_type x1, other arithmetic, per_device(): return out.astype(jnp.bfloat16)  1.54 us

profile of v2, /device:TPU:6, one launch (start us, length us, event | category | flops | bytes accessed | tf_op | source)
XLA Modules:
  0.0 54.4 jit_solution(16162611571909550377)
XLA Ops:
  0.0 52.8 %shard_map.82 = f32[10,2048]{1,0:T(8,128)} custom-call(bf16[10,256]{1,0:T(8,128)(2,1)} %hidden_hbm.1, bf16[256]{0:T(256)(128)(2,1)} %gain_hbm.1, bf16[256,2048]{1,0:T(8,128)(2,1)} %w_query_hbm.1, bf16[256,256]{1,0:T(8,128)(2,1)} %w_keyval_hbm.1, bf16[256,2048]{1,0:T(8,128)(2,1)} %w_output_hbm.1, bf16[10,1,512,128]{3,2,1,0:T(8,128)(2,1)} %key_hbm.1, ...), custom_call_target="tpu_custom_call" | custom-call | tf_op jit(solution)/shard_map/pallas_call | solution.py:330
  52.8 1.5 %convert_element_type.3 = bf16[10,2048]{1,0:T(8,128)(2,1)} convert(f32[10,2048]{1,0:T(8,128)} %shard_map.82) | non-fusion elementwise | flops 20480 | bytes 122880 | tf_op jit(solution)/shard_map/convert_element_type | solution.py:340

commit v3 on v2

--- a/solution.py
+++ b/solution.py
@@ -44,9 +44,9 @@
 
 
 def kernel(
-    hidden_hbm, gain_hbm, w_query_hbm, w_keyval_hbm, w_output_hbm, key_hbm, value_hbm, lengths_ref,
+    hidden_hbm, gain_hbm, w_query_hbm, w_keyval_hbm, w_output_hbm, key_hbm, value_hbm, lengths_hbm,
     out_ref,
-    hidden_in, norm_gain, w_query, w_keyval, w_output, keys, values,
+    hidden_in, norm_gain, w_query, w_keyval, w_output, keys, values, lengths,
     in_send, in_plane, in_mid, in_line, in_sum, in_all,
     soft_send, soft_recv, soft_mid, attn_recv,
     out_send, out_plane, out_mid, out_line, out_sum, out_all,
@@ -67,45 +67,42 @@
     def line_mate(index):
         return (y + offset(index, 8)) % 8
 
-    barrier = pltpu.get_barrier_semaphore()
-
-    def signal(gx_to, gy_to):
-        pl.semaphore_signal(barrier, inc=1, device_id=(gx_to, gy_to), device_id_type=MESH)
-
-    @pl.when(source_gy != gy)
-    def _():
-        def greet_source(index, carry):
-            signal(place(index, y, z), source_gy)
-            return carry
-
-        lax.fori_loop(0, 4, greet_source, 0)
-
-    def greet(index, carry):
-        x_mate, z_mate = plane_mate(index)
-        y_mate = line_mate(index)
-        signal(place(x, y_mate, 1 - z), gy)
-        signal(place(x, y_mate, z), gy)
-        signal(place(x_mate, y, z_mate), gy)
-        return carry
-
-    lax.fori_loop(0, 7, greet, 0)
-
     loads = [
         pltpu.make_async_copy(src, dst, load_sem.at[k])
         for k, (src, dst) in enumerate(
             [
                 (hidden_hbm, hidden_in),
                 (gain_hbm, norm_gain),
-                (w_query_hbm, w_query),
+                (w_query_hbm.at[:, pl.ds(0, 1024)], w_query.at[:, pl.ds(0, 1024)]),
+                (w_query_hbm.at[:, pl.ds(1024, 1024)], w_query.at[:, pl.ds(1024, 1024)]),
                 (w_keyval_hbm, w_keyval),
                 (key_hbm, keys),
                 (value_hbm, values),
                 (w_output_hbm, w_output),
+                (lengths_hbm, lengths),
             ]
         )
     ]
-    for load in loads:
+    for load in loads[:5]:
         load.start()
+
+    barrier = pltpu.get_barrier_semaphore()
+
+    def signal(gx_to, gy_to):
+        pl.semaphore_signal(barrier, inc=1, device_id=(gx_to, gy_to), device_id_type=MESH)
+
+    for index in range(7):
+        x_mate, z_mate = plane_mate(index)
+        signal(place(x_mate, y, z_mate), gy)
+    for index in range(7):
+        y_mate = line_mate(index)
+        signal(place(x, y_mate, 1 - z), gy)
+        signal(place(x, y_mate, z), gy)
+
+    @pl.when(source_gy != gy)
+    def _():
+        for index in range(4):
+            signal(place(index, y, z), source_gy)
 
     def copy(stage, src, dst, gx_to, gy_to):
         pltpu.make_async_remote_copy(
@@ -119,7 +116,10 @@
             copy(stage, send.at[x_mate * 2 + z_mate], by_plane.at[plane], place(x_mate, y, z_mate), gy)
             return carry
 
-        lax.fori_loop(0, 7, to_plane, 0)
+        lax.fori_loop(0, 7, to_plane, 0, unroll=True)
+        if stage == 0:
+            for load in loads[5:]:
+                load.start()
         by_plane[plane] = send[plane]
         await_bytes(by_plane.at[pl.ds(0, 7)], recv_sem.at[stage])
         mid[...] = jnp.sum(by_plane[...], axis=0)
@@ -128,7 +128,7 @@
             copy(stage + 1, mid, by_line.at[y], place(x, line_mate(index), z), gy)
             return carry
 
-        lax.fori_loop(0, 7, to_line, 0)
+        lax.fori_loop(0, 7, to_line, 0, unroll=True)
         by_line[y] = mid[...]
         await_bytes(by_line.at[pl.ds(0, 7)], recv_sem.at[stage + 1])
         total[...] = jnp.sum(by_line[...], axis=0)
@@ -138,7 +138,7 @@
             copy(stage + 2, total, everything.at[plane], place(x_mate, y, z_mate), gy)
             return carry
 
-        lax.fori_loop(0, 7, back_to_plane, 0)
+        lax.fori_loop(0, 7, back_to_plane, 0, unroll=True)
         everything[plane] = total[...]
         await_bytes(everything.at[pl.ds(0, 7)], recv_sem.at[stage + 2])
 
@@ -148,12 +148,15 @@
     squares = jnp.broadcast_to(jnp.sum(hidden * hidden, axis=1, keepdims=True), (ROWS, HD))
     gain = norm_gain[...].astype(jnp.float32).reshape(1, -1)
     scaled_in = (hidden * gain).astype(jnp.bfloat16)
-    loads[2].wait()
-    query_part = jnp.dot(scaled_in, w_query[...], preferred_element_type=jnp.float32)
-    for j in range(SLICES):
-        in_send[j, :ROWS, :] = query_part[:, j * 2 * HD : (j * 2 + 1) * HD]
-        in_send[j, ROWS:PAIR, :] = query_part[:, (j * 2 + 1) * HD : (j * 2 + 2) * HD]
-    loads[3].wait()
+    for part in range(2):
+        loads[2 + part].wait()
+        columns = slice(part * 1024, (part + 1) * 1024)
+        query_part = jnp.dot(scaled_in, w_query[:, columns], preferred_element_type=jnp.float32)
+        for k in range(4):
+            j = part * 4 + k
+            in_send[j, :ROWS, :] = query_part[:, k * 2 * HD : (k * 2 + 1) * HD]
+            in_send[j, ROWS:PAIR, :] = query_part[:, (k * 2 + 1) * HD : (k * 2 + 2) * HD]
+    loads[4].wait()
     keyval_part = jnp.dot(scaled_in, w_keyval[...], preferred_element_type=jnp.float32)
     extras = [keyval_part[:, :HD], keyval_part[:, HD:], squares, jnp.zeros((2, HD), jnp.float32)]
     slot = 0
@@ -176,7 +179,8 @@
         slot = kind * ROWS + r
         return in_all[slot // 4, PAIR + slot % 4 : PAIR + slot % 4 + 1, :]
 
-    loads[4].wait()
+    loads[5].wait()
+    loads[8].wait()
     score_scale = HD ** (-0.5)
     position = gx * SPAN + lax.broadcasted_iota(jnp.int32, (GROUP, SPAN), 1)
     first = gx == 0
@@ -197,13 +201,13 @@
             )
             * score_scale
         )
-    loads[5].wait()
+    loads[6].wait()
     head_row = lax.broadcasted_iota(jnp.int32, (GROUP, HD), 0)
     lane = lax.broadcasted_iota(jnp.int32, (GROUP, HD), 1) - ROWS * (head_row // SLICES)
     peaks = jnp.zeros((GROUP, HD), jnp.float32)
     totals = jnp.zeros((GROUP, HD), jnp.float32)
     for r in range(ROWS):
-        valid = position < lengths_ref[r]
+        valid = position < lengths[r]
         masked = jnp.where(valid, scores[r], -1e30)
         peak = jnp.maximum(jnp.max(masked, axis=1, keepdims=True), scores_new[r])
         weights = jnp.where(valid, jnp.exp(masked - peak), 0.0)
@@ -265,7 +269,7 @@
     accum, _, _, columns = merge_partials(attn_recv, 4)
     attention = (accum[:PAIR] / columns[:PAIR, 4:5]).astype(jnp.bfloat16)
     attention = jnp.concatenate([attention[:ROWS], attention[ROWS:]], axis=1)
-    loads[6].wait()
+    loads[7].wait()
     out_part = jnp.dot(attention, w_output[...], preferred_element_type=jnp.float32)
     for j in range(SLICES):
         out_send[j, :ROWS, :] = out_part[:, j * 2 * HD : (j * 2 + 1) * HD]
@@ -297,7 +301,7 @@
 
 
 def per_device(hidden_in, norm_gain, w_query, w_keyval, w_output, key_cache, value_cache, lengths):
-    hbm = pl.BlockSpec(memory_space=pl.ANY)
+    hbm = pl.BlockSpec(memory_space=pltpu.HBM)
 
     def reduction(rows):
         return [
@@ -317,26 +321,27 @@
         pltpu.VMEM(w_output.shape, jnp.bfloat16),
         pltpu.VMEM(key_cache.shape, jnp.bfloat16),
         pltpu.VMEM(value_cache.shape, jnp.bfloat16),
+        pltpu.SMEM(lengths.shape, jnp.int32),
         *reduction(BLOCK),
         pltpu.VMEM((SLICES, BLOCK, HD), jnp.float32),
         pltpu.VMEM((16, BLOCK, HD), jnp.float32),
         pltpu.VMEM((BLOCK, HD), jnp.float32),
         pltpu.VMEM((4, BLOCK, HD), jnp.float32),
         *reduction(PAIR),
-        pltpu.SemaphoreType.DMA((7,)),
+        pltpu.SemaphoreType.DMA((9,)),
         pltpu.SemaphoreType.DMA((8,)),
         pltpu.SemaphoreType.DMA((8,)),
     ]
     out = pl.pallas_call(
         kernel,
         out_shape=jax.ShapeDtypeStruct((ROWS, GROUP * HD), jnp.float32),
-        in_specs=[hbm] * 7 + [pl.BlockSpec(memory_space=pltpu.SMEM)],
+        in_specs=[hbm] * 8,
         out_specs=pl.BlockSpec(memory_space=pltpu.VMEM),
         scratch_shapes=scratch,
         compiler_params=pltpu.CompilerParams(
-            collective_id=0, has_side_effects=True, vmem_limit_bytes=60 * 2**20
+            collective_id=0, has_side_effects=True, vmem_limit_bytes=16 * 2**20
         ),
-    )(hidden_in, norm_gain, w_query, w_keyval, w_output, key_cache, value_cache, lengths)
+    )(*[pltpu.with_memory_space_constraint(a, pltpu.HBM) for a in (hidden_in, norm_gain, w_query, w_keyval, w_output, key_cache, value_cache, lengths)])
     return out.astype(jnp.bfloat16)
 
 

time: 54.5 us -> 52.5 us (0.963)
  Pallas kernels: 52.8 us -> 51.7 us
  other arithmetic: 1.54 us -> 0.64 us
    pallas_call x1, Pallas kernels: 52.8 us -> 51.7 us  [per_device(): pl.pallas_call(kernel, out_shape=jax.ShapeDtypeStruct((ROWS, GROUP * HD),...]
    convert_element_type x1, other arithmetic: 1.54 us -> 0.64 us  [per_device(): return out.astype(jnp.bfloat16)]
where the time goes in v3:
time: 52.5 us; the launch traced here: 52.4 us
  Pallas kernels  51.7 us (98%)
  other arithmetic  0.64 us (1%)
    pallas_call x1, Pallas kernels, per_device(): pl.pallas_call(kernel, out_shape=jax.ShapeDtypeStruct((ROWS, GROUP * HD),...  51.7 us

profile of v3, /device:TPU:6, one launch (start us, length us, event | category | flops | bytes accessed | tf_op | source)
XLA Modules:
  0.0 52.4 jit_solution(2975400453800161467)
XLA Ops:
  0.0 51.7 %shard_map.82 = f32[10,2048]{1,0:T(8,128)S(1)} custom-call(bf16[10,256]{1,0:T(8,128)(2,1)} %hidden_hbm.1, bf16[256]{0:T(256)(128)(2,1)} %gain_hbm.1, bf16[256,2048]{1,0:T(8,128)(2,1)} %w_query_hbm.1, bf16[256,256]{1,0:T(8,128)(2,1)} %w_keyval_hbm.1, bf16[256,2048]{1,0:T(8,128)(2,1)} %w_output_hbm.1, bf16[10,1,512,128]{3,2,1,0:T(8,128)(2,1)} %key_hbm.1, ...), custom_call_target="tpu_custom_call" | custom-call | tf_op jit(solution)/shard_map/pallas_call | solution.py:335
  51.7 0.6 %convert_element_type.3 = bf16[10,2048]{1,0:T(8,128)(2,1)} convert(f32[10,2048]{1,0:T(8,128)S(1)} %shard_map.82) | non-fusion elementwise | flops 20480 | bytes 122880 | tf_op jit(solution)/shard_map/convert_element_type | solution.py:345

commit v4 on v3

--- a/solution.py
+++ b/solution.py
@@ -17,8 +17,9 @@
 SLICES = 8
 PAIR = 2 * ROWS
 BLOCK = PAIR + 4
+SOFT = 32
 PEAK = PAIR
-TOTAL = PAIR + 1
+TOTAL = PEAK + 3
 
 
 def offset(index, size):
@@ -29,26 +30,36 @@
     pltpu.make_async_copy(ref, ref, sem).wait()
 
 
+def split(value):
+    high = value.astype(jnp.bfloat16).astype(jnp.float32)
+    rest = value - high
+    middle = rest.astype(jnp.bfloat16).astype(jnp.float32)
+    return high, middle, rest - middle
+
+
 def merge_partials(blocks, count):
-    peaks = blocks[:, PEAK, :]
+    def joined(row):
+        return blocks[:count, row, :] + blocks[:count, row + 1, :] + blocks[:count, row + 2, :]
+
+    peaks = joined(PEAK)
     peak = jnp.max(peaks, axis=0, keepdims=True)
     factors = jnp.exp(peaks - peak)
-    total = jnp.sum(factors * blocks[:, TOTAL, :], axis=0, keepdims=True)
+    total = jnp.sum(factors * joined(TOTAL), axis=0, keepdims=True)
     if count < 8:
         factors = jnp.concatenate([factors, jnp.broadcast_to(total, (8 - count, HD))], axis=0)
     columns = jnp.transpose(factors)
-    accum = columns[:BLOCK, 0:1] * blocks[0]
+    accum = columns[:BLOCK, 0:1] * blocks[0, :BLOCK]
     for k in range(1, count):
-        accum = accum + columns[:BLOCK, k : k + 1] * blocks[k]
+        accum = accum + columns[:BLOCK, k : k + 1] * blocks[k, :BLOCK]
     return accum, peak, total, columns
 
 
 def kernel(
     hidden_hbm, gain_hbm, w_query_hbm, w_keyval_hbm, w_output_hbm, key_hbm, value_hbm, lengths_hbm,
     out_ref,
-    hidden_in, norm_gain, w_query, w_keyval, w_output, keys, values, lengths,
+    hidden_in, norm_gain, w_query, w_keyval, w_output, keys, values, lengths, keys_across,
     in_send, in_plane, in_mid, in_line, in_sum, in_all,
-    soft_send, soft_recv, soft_mid, attn_recv,
+    soft_wide, soft_send, soft_recv, soft_mid, attn_recv,
     out_send, out_plane, out_mid, out_line, out_sum, out_all,
     load_sem, send_sem, recv_sem,
 ):
@@ -83,26 +94,26 @@
             ]
         )
     ]
-    for load in loads[:5]:
-        load.start()
 
     barrier = pltpu.get_barrier_semaphore()
 
     def signal(gx_to, gy_to):
         pl.semaphore_signal(barrier, inc=1, device_id=(gx_to, gy_to), device_id_type=MESH)
+
+    @pl.when(source_gy != gy)
+    def _():
+        for index in range(4):
+            signal(place(index, y, z), source_gy)
 
     for index in range(7):
         x_mate, z_mate = plane_mate(index)
         signal(place(x_mate, y, z_mate), gy)
     for index in range(7):
         y_mate = line_mate(index)
-        signal(place(x, y_mate, 1 - z), gy)
         signal(place(x, y_mate, z), gy)
 
-    @pl.when(source_gy != gy)
-    def _():
-        for index in range(4):
-            signal(place(index, y, z), source_gy)
+    for load in loads[:5]:
+        load.start()
 
     def copy(stage, src, dst, gx_to, gy_to):
         pltpu.make_async_remote_copy(
@@ -129,6 +140,10 @@
             return carry
 
         lax.fori_loop(0, 7, to_line, 0, unroll=True)
+        if stage == 0:
+            loads[5].wait()
+            for r in range(ROWS):
+                keys_across[r] = jnp.transpose(keys[r, 0])
         by_line[y] = mid[...]
         await_bytes(by_line.at[pl.ds(0, 7)], recv_sem.at[stage + 1])
         total[...] = jnp.sum(by_line[...], axis=0)
@@ -167,11 +182,11 @@
 
     @pl.when(merges)
     def _():
-        pl.semaphore_wait(barrier, 21 + 7)
+        pl.semaphore_wait(barrier, 14 + 7)
 
     @pl.when(jnp.logical_not(merges))
     def _():
-        pl.semaphore_wait(barrier, 21)
+        pl.semaphore_wait(barrier, 14)
 
     all_reduce(0, in_send, in_plane, in_mid, in_line, in_sum, in_all)
 
@@ -179,7 +194,6 @@
         slot = kind * ROWS + r
         return in_all[slot // 4, PAIR + slot % 4 : PAIR + slot % 4 + 1, :]
 
-    loads[5].wait()
     loads[8].wait()
     score_scale = HD ** (-0.5)
     position = gx * SPAN + lax.broadcasted_iota(jnp.int32, (GROUP, SPAN), 1)
@@ -196,9 +210,7 @@
         )
         scores_new.append(jnp.where(first, score_new, -1e30))
         scores.append(
-            lax.dot_general(
-                query, keys[r, 0], (((1,), (1,)), ((), ())), preferred_element_type=jnp.float32
-            )
+            jnp.dot(query, keys_across[r], preferred_element_type=jnp.float32)
             * score_scale
         )
     loads[6].wait()
@@ -217,14 +229,15 @@
             weights.astype(jnp.bfloat16), values[r, 0], preferred_element_type=jnp.float32
         )
         accum = accum + fresh * values_new[r]
-        soft_send[:, r, :] = accum[:SLICES]
-        soft_send[:, ROWS + r, :] = accum[SLICES:]
+        soft_wide[:SLICES, r, :] = accum[:SLICES]
+        soft_wide[:SLICES, ROWS + r, :] = accum[SLICES:]
         peaks = jnp.where(lane == r, peak, peaks)
         totals = jnp.where(lane == r, total, totals)
-    soft_send[:, PEAK, :] = peaks[:SLICES] + peaks[SLICES:]
-    soft_send[:, TOTAL, :] = totals[:SLICES] + totals[SLICES:]
-    soft_send[:, TOTAL + 1, :] = jnp.zeros((SLICES, HD), jnp.float32)
-    soft_send[:, TOTAL + 2, :] = jnp.zeros((SLICES, HD), jnp.float32)
+    terms = split(peaks[:SLICES] + peaks[SLICES:]) + split(totals[:SLICES] + totals[SLICES:])
+    for k in range(SOFT - PEAK):
+        term = terms[k] if k < 6 else jnp.zeros((SLICES, HD), jnp.float32)
+        soft_wide[:SLICES, PEAK + k, :] = term
+    soft_send[...] = soft_wide[:SLICES].astype(jnp.bfloat16)
 
     def to_merger(index, carry):
         y_to, z_to = (gy % 2) * 4 + index // 2, index % 2
@@ -241,13 +254,17 @@
     def _():
         soft_recv[y * 2 + z] = soft_send[(y % 4) * 2 + z]
         await_bytes(soft_recv.at[pl.ds(0, 15)], recv_sem.at[3])
-        accum, peak, total, _ = merge_partials(soft_recv, 16)
-        soft_mid[...] = accum
-        soft_mid[PEAK : PEAK + 1, :] = peak
-        soft_mid[TOTAL : TOTAL + 1, :] = total
+        soft_wide[...] = soft_recv[...].astype(jnp.float32)
+        accum, peak, total, _ = merge_partials(soft_wide, 16)
+        merged = soft_wide.at[0]
+        merged[:BLOCK, :] = accum
+        merged[BLOCK:, :] = jnp.zeros((SOFT - BLOCK, HD), jnp.float32)
+        for k, term in enumerate(split(peak) + split(total)):
+            merged[PEAK + k : PEAK + k + 1, :] = term
+        soft_mid[...] = merged[...].astype(jnp.bfloat16)
 
         def to_outputs(index, carry):
-            gy_to = (gy + 4 + index) % 8
+            gy_to = index
 
             @pl.when((gy_to != gy) | (x != gy // 2))
             def _():
@@ -266,7 +283,8 @@
     def _():
         await_bytes(attn_recv, recv_sem.at[4])
 
-    accum, _, _, columns = merge_partials(attn_recv, 4)
+    soft_wide[:4] = attn_recv[...].astype(jnp.float32)
+    accum, _, _, columns = merge_partials(soft_wide, 4)
     attention = (accum[:PAIR] / columns[:PAIR, 4:5]).astype(jnp.bfloat16)
     attention = jnp.concatenate([attention[:ROWS], attention[ROWS:]], axis=1)
     loads[7].wait()
@@ -322,11 +340,13 @@
         pltpu.VMEM(key_cache.shape, jnp.bfloat16),
         pltpu.VMEM(value_cache.shape, jnp.bfloat16),
         pltpu.SMEM(lengths.shape, jnp.int32),
+        pltpu.VMEM((ROWS, HD, SPAN), jnp.bfloat16),
         *reduction(BLOCK),
-        pltpu.VMEM((SLICES, BLOCK, HD), jnp.float32),
-        pltpu.VMEM((16, BLOCK, HD), jnp.float32),
-        pltpu.VMEM((BLOCK, HD), jnp.float32),
-        pltpu.VMEM((4, BLOCK, HD), jnp.float32),
+        pltpu.VMEM((16, SOFT, HD), jnp.float32),
+        pltpu.VMEM((SLICES, SOFT, HD), jnp.bfloat16),
+        pltpu.VMEM((16, SOFT, HD), jnp.bfloat16),
+        pltpu.VMEM((SOFT, HD), jnp.bfloat16),
+        pltpu.VMEM((4, SOFT, HD), jnp.bfloat16),
         *reduction(PAIR),
         pltpu.SemaphoreType.DMA((9,)),
         pltpu.SemaphoreType.DMA((8,)),

time: 52.5 us -> 50.9 us (0.970)
  Pallas kernels: 51.7 us -> 50.1 us
    pallas_call x1, Pallas kernels: 51.7 us -> 50.1 us  [per_device(): pl.pallas_call(kernel, out_shape=jax.ShapeDtypeStruct((ROWS, GROUP * HD),...]
where the time goes in v4:
time: 50.9 us; the launch traced here: 50.8 us
  Pallas kernels  50.1 us (98%)
  other arithmetic  0.64 us (1%)
    pallas_call x1, Pallas kernels, per_device(): pl.pallas_call(kernel, out_shape=jax.ShapeDtypeStruct((ROWS, GROUP * HD),...  50.1 us

profile of v4, /device:TPU:6, one launch (start us, length us, event | category | flops | bytes accessed | tf_op | source)
XLA Modules:
  0.0 50.8 jit_solution(18168582026922576819)
XLA Ops:
  0.0 50.1 %shard_map.82 = f32[10,2048]{1,0:T(8,128)S(1)} custom-call(bf16[10,256]{1,0:T(8,128)(2,1)} %hidden_hbm.1, bf16[256]{0:T(256)(128)(2,1)} %gain_hbm.1, bf16[256,2048]{1,0:T(8,128)(2,1)} %w_query_hbm.1, bf16[256,256]{1,0:T(8,128)(2,1)} %w_keyval_hbm.1, bf16[256,2048]{1,0:T(8,128)(2,1)} %w_output_hbm.1, bf16[10,1,512,128]{3,2,1,0:T(8,128)(2,1)} %key_hbm.1, ...), custom_call_target="tpu_custom_call" | custom-call | tf_op jit(solution)/shard_map/pallas_call | solution.py:355
  50.2 0.6 %convert_element_type.3 = bf16[10,2048]{1,0:T(8,128)(2,1)} convert(f32[10,2048]{1,0:T(8,128)S(1)} %shard_map.82) | non-fusion elementwise | flops 20480 | bytes 122880 | tf_op jit(solution)/shard_map/convert_element_type | solution.py:365

commit v5 on v4

--- a/solution.py
+++ b/solution.py
@@ -61,13 +61,16 @@
     in_send, in_plane, in_mid, in_line, in_sum, in_all,
     soft_wide, soft_send, soft_recv, soft_mid, attn_recv,
     out_send, out_plane, out_mid, out_line, out_sum, out_all,
-    load_sem, send_sem, recv_sem,
+    load_sem, send_sem, recv_sem, late_sem,
 ):
     gx, gy = lax.axis_index("gx"), lax.axis_index("gy")
     x, y, z = gx // 16, (gx // 2) % 8, gx % 2
     plane = x * 2 + z
     merges = y // 4 == gy % 2
     source_gy = 2 * x + y // 4
+
+    def is_late(y):
+        return (y + 5) % 8 < 4
 
     def place(x, y, z):
         return x * 16 + y * 2 + z
@@ -102,15 +105,17 @@
 
     @pl.when(source_gy != gy)
     def _():
-        for index in range(4):
-            signal(place(index, y, z), source_gy)
+        signal(gx, source_gy)
 
     for index in range(7):
         x_mate, z_mate = plane_mate(index)
         signal(place(x_mate, y, z_mate), gy)
     for index in range(7):
         y_mate = line_mate(index)
-        signal(place(x, y_mate, z), gy)
+
+        @pl.when(is_late(y_mate) | jnp.logical_not(is_late(y)))
+        def _():
+            signal(place(x, y_mate, z), gy)
 
     for load in loads[:5]:
         load.start()
@@ -134,6 +139,11 @@
         by_plane[plane] = send[plane]
         await_bytes(by_plane.at[pl.ds(0, 7)], recv_sem.at[stage])
         mid[...] = jnp.sum(by_plane[...], axis=0)
+        if stage == 0:
+
+            @pl.when(jnp.logical_not(is_late(y)))
+            def _():
+                pl.semaphore_wait(late_sem, 4)
 
         def to_line(index, carry):
             copy(stage + 1, mid, by_line.at[y], place(x, line_mate(index), z), gy)
@@ -180,13 +190,15 @@
             in_send[slot // 4, PAIR + slot % 4 : PAIR + slot % 4 + 1, :] = extra[r : r + 1]
             slot += 1
 
-    @pl.when(merges)
-    def _():
-        pl.semaphore_wait(barrier, 14 + 7)
-
-    @pl.when(jnp.logical_not(merges))
-    def _():
-        pl.semaphore_wait(barrier, 14)
+    greetings = 10 + 4 * is_late(y).astype(jnp.int32) + 7 * (source_gy == gy).astype(jnp.int32)
+    pl.semaphore_wait(barrier, greetings)
+
+    @pl.when(is_late(y))
+    def _():
+        for y_mate in (0, 1, 7, 2):
+            pl.semaphore_signal(
+                late_sem, inc=1, device_id=(place(x, y_mate, z), gy), device_id_type=MESH
+            )
 
     all_reduce(0, in_send, in_plane, in_mid, in_line, in_sum, in_all)
 
@@ -351,6 +363,7 @@
         pltpu.SemaphoreType.DMA((9,)),
         pltpu.SemaphoreType.DMA((8,)),
         pltpu.SemaphoreType.DMA((8,)),
+        pltpu.SemaphoreType.REGULAR,
     ]
     out = pl.pallas_call(
         kernel,

time: 50.9 us -> 50 us (0.982)
  Pallas kernels: 50.1 us -> 49.2 us
    pallas_call x1, Pallas kernels: 50.1 us -> 49.2 us  [per_device(): pl.pallas_call(kernel, out_shape=jax.ShapeDtypeStruct((ROWS, GROUP * HD),...]
where the time goes in v5:
time: 50 us; the launch traced here: 49.9 us
  Pallas kernels  49.2 us (98%)
  other arithmetic  0.64 us (1%)
    pallas_call x1, Pallas kernels, per_device(): pl.pallas_call(kernel, out_shape=jax.ShapeDtypeStruct((ROWS, GROUP * HD),...  49.2 us

profile of v5, /device:TPU:6, one launch (start us, length us, event | category | flops | bytes accessed | tf_op | source)
XLA Modules:
  0.0 49.9 jit_solution(16941199916098226389)
XLA Ops:
  0.0 49.2 %shard_map.82 = f32[10,2048]{1,0:T(8,128)S(1)} custom-call(bf16[10,256]{1,0:T(8,128)(2,1)} %hidden_hbm.1, bf16[256]{0:T(256)(128)(2,1)} %gain_hbm.1, bf16[256,2048]{1,0:T(8,128)(2,1)} %w_query_hbm.1, bf16[256,256]{1,0:T(8,128)(2,1)} %w_keyval_hbm.1, bf16[256,2048]{1,0:T(8,128)(2,1)} %w_output_hbm.1, bf16[10,1,512,128]{3,2,1,0:T(8,128)(2,1)} %key_hbm.1, ...), custom_call_target="tpu_custom_call" | custom-call | tf_op jit(solution)/shard_map/pallas_call | solution.py:368
  49.3 0.6 %convert_element_type.3 = bf16[10,2048]{1,0:T(8,128)(2,1)} convert(f32[10,2048]{1,0:T(8,128)S(1)} %shard_map.82) | non-fusion elementwise | flops 20480 | bytes 122880 | tf_op jit(solution)/shard_map/convert_element_type | solution.py:378

commit v6 on v5

--- a/solution.py
+++ b/solution.py
@@ -234,7 +234,8 @@
         valid = position < lengths[r]
         masked = jnp.where(valid, scores[r], -1e30)
         peak = jnp.maximum(jnp.max(masked, axis=1, keepdims=True), scores_new[r])
-        weights = jnp.where(valid, jnp.exp(masked - peak), 0.0)
+        peak = jnp.maximum(peak, -1e29)
+        weights = jnp.exp(masked - peak)
         fresh = jnp.where(first, jnp.exp(scores_new[r] - peak), 0.0)
         total = jnp.sum(weights, axis=1, keepdims=True) + fresh
         accum = jnp.dot(
@@ -251,16 +252,16 @@
         soft_wide[:SLICES, PEAK + k, :] = term
     soft_send[...] = soft_wide[:SLICES].astype(jnp.bfloat16)
 
-    def to_merger(index, carry):
-        y_to, z_to = (gy % 2) * 4 + index // 2, index % 2
-
-        @pl.when((y_to != y) | (z_to != z))
-        def _():
-            copy(3, soft_send.at[index], soft_recv.at[y * 2 + z], place(x, y_to, z_to), gy)
-
-        return carry
-
-    lax.fori_loop(0, SLICES, to_merger, 0)
+    for index in range(8):
+        y_to = (y + offset(index, 8)) % 8
+        for z_step in (1, 0):
+            if index == 7 and z_step == 0:
+                continue
+            z_to = (z + z_step) % 2
+
+            @pl.when(y_to // 4 == gy % 2)
+            def _():
+                copy(3, soft_send.at[(y_to % 4) * 2 + z_to], soft_recv.at[y * 2 + z], place(x, y_to, z_to), gy)
 
     @pl.when(merges)
     def _():
@@ -284,7 +285,7 @@
 
             return carry
 
-        lax.fori_loop(0, 8, to_outputs, 0)
+        lax.fori_loop(0, 8, to_outputs, 0, unroll=True)
 
     @pl.when(source_gy == gy)
     def _():

time: 50 us -> 49.6 us (level)
  no operation moved by 1% of the time
where the time goes in v6:
time: 49.6 us; the launch traced here: 49.4 us
  Pallas kernels  48.8 us (98%)
  other arithmetic  0.64 us (1%)
    pallas_call x1, Pallas kernels, per_device(): pl.pallas_call(kernel, out_shape=jax.ShapeDtypeStruct((ROWS, GROUP * HD),...  48.8 us

profile of v6, /device:TPU:6, one launch (start us, length us, event | category | flops | bytes accessed | tf_op | source)
XLA Modules:
  0.0 49.4 jit_solution(12248616193958242857)
XLA Ops:
  0.0 48.8 %shard_map.82 = f32[10,2048]{1,0:T(8,128)S(1)} custom-call(bf16[10,256]{1,0:T(8,128)(2,1)} %hidden_hbm.1, bf16[256]{0:T(256)(128)(2,1)} %gain_hbm.1, bf16[256,2048]{1,0:T(8,128)(2,1)} %w_query_hbm.1, bf16[256,256]{1,0:T(8,128)(2,1)} %w_keyval_hbm.1, bf16[256,2048]{1,0:T(8,128)(2,1)} %w_output_hbm.1, bf16[10,1,512,128]{3,2,1,0:T(8,128)(2,1)} %key_hbm.1, ...), custom_call_target="tpu_custom_call" | custom-call | tf_op jit(solution)/shard_map/pallas_call | solution.py:369
  48.8 0.6 %convert_element_type.3 = bf16[10,2048]{1,0:T(8,128)(2,1)} convert(f32[10,2048]{1,0:T(8,128)S(1)} %shard_map.82) | non-fusion elementwise | flops 20480 | bytes 122880 | tf_op jit(solution)/shard_map/convert_element_type | solution.py:379

commit v7 on v6

--- a/solution.py
+++ b/solution.py
@@ -127,12 +127,14 @@
         ).start()
 
     def all_reduce(stage, send, by_plane, mid, by_line, total, everything):
-        def to_plane(index, carry):
-            x_mate, z_mate = plane_mate(index)
-            copy(stage, send.at[x_mate * 2 + z_mate], by_plane.at[plane], place(x_mate, y, z_mate), gy)
-            return carry
-
-        lax.fori_loop(0, 7, to_plane, 0, unroll=True)
+        if stage == 0:
+
+            def to_plane(index, carry):
+                x_mate, z_mate = plane_mate(index)
+                copy(stage, send.at[x_mate * 2 + z_mate], by_plane.at[plane], place(x_mate, y, z_mate), gy)
+                return carry
+
+            lax.fori_loop(0, 7, to_plane, 0, unroll=True)
         if stage == 0:
             for load in loads[5:]:
                 load.start()
@@ -305,6 +307,11 @@
     for j in range(SLICES):
         out_send[j, :ROWS, :] = out_part[:, j * 2 * HD : (j * 2 + 1) * HD]
         out_send[j, ROWS:, :] = out_part[:, (j * 2 + 1) * HD : (j * 2 + 2) * HD]
+
+        @pl.when(j != plane)
+        def _():
+            copy(5, out_send.at[j], out_plane.at[plane], place(j // 2, y, j % 2), gy)
+
     all_reduce(5, out_send, out_plane, out_mid, out_line, out_sum, out_all)
     for j in range(SLICES):
         out_ref[:, j * 2 * HD : (j * 2 + 1) * HD] = out_all[j, :ROWS, :]

time: 49.6 us -> 49.5 us (level)
  no operation moved by 1% of the time
where the time goes in v7:
time: 49.5 us; the launch traced here: 49.3 us
  Pallas kernels  48.7 us (98%)
  other arithmetic  0.64 us (1%)
    pallas_call x1, Pallas kernels, per_device(): pl.pallas_call(kernel, out_shape=jax.ShapeDtypeStruct((ROWS, GROUP * HD),...  48.7 us

profile of v7, /device:TPU:6, one launch (start us, length us, event | category | flops | bytes accessed | tf_op | source)
XLA Modules:
  0.0 49.3 jit_solution(15255414042469384200)
XLA Ops:
  0.0 48.7 %shard_map.82 = f32[10,2048]{1,0:T(8,128)S(1)} custom-call(bf16[10,256]{1,0:T(8,128)(2,1)} %hidden_hbm.1, bf16[256]{0:T(256)(128)(2,1)} %gain_hbm.1, bf16[256,2048]{1,0:T(8,128)(2,1)} %w_query_hbm.1, bf16[256,256]{1,0:T(8,128)(2,1)} %w_keyval_hbm.1, bf16[256,2048]{1,0:T(8,128)(2,1)} %w_output_hbm.1, bf16[10,1,512,128]{3,2,1,0:T(8,128)(2,1)} %key_hbm.1, ...), custom_call_target="tpu_custom_call" | custom-call | tf_op jit(solution)/shard_map/pallas_call | solution.py:376
  48.7 0.6 %convert_element_type.3 = bf16[10,2048]{1,0:T(8,128)(2,1)} convert(f32[10,2048]{1,0:T(8,128)S(1)} %shard_map.82) | non-fusion elementwise | flops 20480 | bytes 122880 | tf_op jit(solution)/shard_map/convert_element_type | solution.py:386

commit v8 on v7

--- a/solution.py
+++ b/solution.py
@@ -60,7 +60,7 @@
     hidden_in, norm_gain, w_query, w_keyval, w_output, keys, values, lengths, keys_across,
     in_send, in_plane, in_mid, in_line, in_sum, in_all,
     soft_wide, soft_send, soft_recv, soft_mid, attn_recv,
-    out_send, out_plane, out_mid, out_line, out_sum, out_all,
+    out_send, out_plane, out_mid, out_line, out_sum,
     load_sem, send_sem, recv_sem, late_sem,
 ):
     gx, gy = lax.axis_index("gx"), lax.axis_index("gy")
@@ -158,16 +158,30 @@
                 keys_across[r] = jnp.transpose(keys[r, 0])
         by_line[y] = mid[...]
         await_bytes(by_line.at[pl.ds(0, 7)], recv_sem.at[stage + 1])
-        total[...] = jnp.sum(by_line[...], axis=0)
+        summed = jnp.sum(by_line[...], axis=0)
+        if stage == 0:
+            total[...] = summed
+        else:
+            total[:, :HD] = summed[:ROWS]
+            total[:, HD:] = summed[ROWS:]
+
+        def slice_of(ref):
+            if stage == 0:
+                return ref.at[plane]
+            return ref.at[:, pl.ds(pl.multiple_of(plane * 2 * HD, 2 * HD), 2 * HD)]
+
+        def mates_of(ref):
+            return ref.at[pl.ds(0, 7)] if stage == 0 else ref.at[:, pl.ds(0, 7 * 2 * HD)]
+
 
         def back_to_plane(index, carry):
             x_mate, z_mate = plane_mate(index)
-            copy(stage + 2, total, everything.at[plane], place(x_mate, y, z_mate), gy)
+            copy(stage + 2, total, slice_of(everything), place(x_mate, y, z_mate), gy)
             return carry
 
         lax.fori_loop(0, 7, back_to_plane, 0, unroll=True)
-        everything[plane] = total[...]
-        await_bytes(everything.at[pl.ds(0, 7)], recv_sem.at[stage + 2])
+        slice_of(everything)[...] = total[...]
+        await_bytes(mates_of(everything), recv_sem.at[stage + 2])
 
     loads[0].wait()
     loads[1].wait()
@@ -312,14 +326,12 @@
         def _():
             copy(5, out_send.at[j], out_plane.at[plane], place(j // 2, y, j % 2), gy)
 
-    all_reduce(5, out_send, out_plane, out_mid, out_line, out_sum, out_all)
-    for j in range(SLICES):
-        out_ref[:, j * 2 * HD : (j * 2 + 1) * HD] = out_all[j, :ROWS, :]
-        out_ref[:, (j * 2 + 1) * HD : (j * 2 + 2) * HD] = out_all[j, ROWS:, :]
+    all_reduce(5, out_send, out_plane, out_mid, out_line, out_sum, out_ref)
 
     for stage in range(3):
         await_bytes(in_all.at[pl.ds(0, 7)], send_sem.at[stage])
-        await_bytes(out_all.at[pl.ds(0, 7)], send_sem.at[5 + stage])
+        sent = out_line.at[pl.ds(0, 7)] if stage < 2 else out_ref.at[:, pl.ds(0, 7 * 2 * HD)]
+        await_bytes(sent, send_sem.at[5 + stage])
 
     @pl.when(merges)
     def _():
@@ -367,7 +379,8 @@
         pltpu.VMEM((16, SOFT, HD), jnp.bfloat16),
         pltpu.VMEM((SOFT, HD), jnp.bfloat16),
         pltpu.VMEM((4, SOFT, HD), jnp.bfloat16),
-        *reduction(PAIR),
+        *reduction(PAIR)[:4],
+        pltpu.VMEM((ROWS, 2 * HD), jnp.float32),
         pltpu.SemaphoreType.DMA((9,)),
         pltpu.SemaphoreType.DMA((8,)),
         pltpu.SemaphoreType.DMA((8,)),

time: 49.5 us -> 49.6 us (level)
  no operation moved by 1% of the time
where the time goes in v8:
time: 49.6 us; the launch traced here: 49.5 us
  Pallas kernels  48.8 us (98%)
  other arithmetic  0.64 us (1%)
    pallas_call x1, Pallas kernels, per_device(): pl.pallas_call(kernel, out_shape=jax.ShapeDtypeStruct((ROWS, GROUP * HD),...  48.8 us

profile of v8, /device:TPU:6, one launch (start us, length us, event | category | flops | bytes accessed | tf_op | source)
XLA Modules:
  0.0 49.5 jit_solution(10441933821374971565)
XLA Ops:
  0.0 48.8 %shard_map.82 = f32[10,2048]{1,0:T(8,128)S(1)} custom-call(bf16[10,256]{1,0:T(8,128)(2,1)} %hidden_hbm.1, bf16[256]{0:T(256)(128)(2,1)} %gain_hbm.1, bf16[256,2048]{1,0:T(8,128)(2,1)} %w_query_hbm.1, bf16[256,256]{1,0:T(8,128)(2,1)} %w_keyval_hbm.1, bf16[256,2048]{1,0:T(8,128)(2,1)} %w_output_hbm.1, bf16[10,1,512,128]{3,2,1,0:T(8,128)(2,1)} %key_hbm.1, ...), custom_call_target="tpu_custom_call" | custom-call | tf_op jit(solution)/shard_map/pallas_call | solution.py:389
  48.8 0.6 %convert_element_type.3 = bf16[10,2048]{1,0:T(8,128)(2,1)} convert(f32[10,2048]{1,0:T(8,128)S(1)} %shard_map.82) | non-fusion elementwise | flops 20480 | bytes 122880 | tf_op jit(solution)/shard_map/convert_element_type | solution.py:399
